TPU v7x, 512 devices: a whole 4x4x16 slice. The times are simulated.
512 devices in a mesh: row: 32 (over x, y, core), col: 16 (over z).
Axes of the slice: x: 4, y: 4, z: 16, core: 2. Of those that a mesh axis runs over, the one named last changes fastest.
Arguments:
- diag_factor: float32 [1024, 1024], P('row', 'col'), may hold values from -1 to 2.5, as said below
- panel_factor: float32 [16384, 1024], P('row', 'col'), may hold values from -0.046875 to 0.046875
- left_factor: float32 [16384, 8192], P('row', 'col'), may hold values from -0.046875 to 0.046875
- pivot_factor: float32 [1024, 8192], P('row', 'col'), may hold values from -0.1875 to 0.1875
- panel_adjoint: float32 [16384, 1024], P('row', 'col'), may hold values from -6 to 6
- left_adjoint: float32 [16384, 8192], P('row', 'col'), may hold values from -6 to 6
- pivot_adjoint: float32 [1024, 8192], P('row', 'col'), may hold values from -6 to 6
- diag_adjoint: float32 [1024, 1024], P('row', 'col'), may hold values from -6 to 6
Outputs:
- solved_panel: float32 [16384, 1024], P('row', 'col')
- left_out: float32 [16384, 8192], P('row', 'col')
- pivot_out: float32 [1024, 8192], P('row', 'col')
- diag_out: float32 [1024, 1024], P('row', 'col')
Inputs may be any that keep to these rules, and one draw needn't show every extreme that they name: diag_factor is lower triangular: zero above the diagonal, diagonal entries at least 1.
All inputs are finite; a program needn't handle non-finite values.
Results may differ from a plain program's by a relative error of at most 0.000073.
Values sent between devices are 32-bit elements; how exact they have to be, the bound alone decides.
A program may use at most 64 MiB of HBM per device.

v0:
```python
import jax
import jax.numpy as jnp
from jax import lax
from jax.sharding import PartitionSpec as P


def right_solve(tile, source):
    return jax.scipy.linalg.solve_triangular(tile, source.T, trans="T", lower=True).T


def local(
    diag_factor,
    panel_factor,
    left_factor,
    pivot_factor,
    panel_adjoint,
    left_adjoint,
    pivot_adjoint,
    diag_adjoint,
):
    highest = lax.Precision.HIGHEST
    block_width = panel_adjoint.shape[1]
    my_col = lax.axis_index("col")
    my_row = lax.axis_index("row")
    column_block = lax.all_gather(diag_factor, "row", axis=0, tiled=True)
    whole_diag = lax.all_gather(column_block, "col", axis=1, tiled=True)
    full_rows = lax.all_gather(panel_adjoint, "col", axis=1, tiled=True)
    solved = right_solve(whole_diag, full_rows)
    solved_panel = lax.dynamic_slice_in_dim(solved, my_col * block_width, block_width, 1)
    picked = solved
    left_out = left_adjoint - jnp.dot(
        picked,
        lax.all_gather(pivot_factor, "row", axis=0, tiled=True),
        precision=highest,
        preferred_element_type=jnp.float32,
    )
    own_rows = diag_adjoint.shape[0]
    picked = solved
    pivot_sum = lax.psum_scatter(
        jnp.einsum("rk,rc->kc", picked, left_factor, precision=highest),
        "row",
        scatter_dimension=0,
        tiled=True,
    )
    picked = solved
    square_sum = lax.psum_scatter(
        jnp.einsum("rk,rc->kc", picked, panel_factor, precision=highest),
        "row",
        scatter_dimension=0,
        tiled=True,
    )
    pivot_out = pivot_adjoint - pivot_sum
    global_row = my_row * own_rows + lax.broadcasted_iota(jnp.int32, (own_rows, block_width), 0)
    global_col = my_col * block_width + lax.broadcasted_iota(jnp.int32, (own_rows, block_width), 1)
    diag_out = diag_adjoint - jnp.where(global_col <= global_row, square_sum, 0.0)
    return (solved_panel, left_out, pivot_out, diag_out)


def solution(mesh):
    in_specs = (
        P("row", "col"),
        P("row", "col"),
        P("row", "col"),
        P("row", "col"),
        P("row", "col"),
        P("row", "col"),
        P("row", "col"),
        P("row", "col"),
    )
    out_specs = (P("row", "col"), P("row", "col"), P("row", "col"), P("row", "col"))
    return jax.shard_map(local, mesh=mesh, in_specs=in_specs, out_specs=out_specs, check_vma=False)
```

profile of v0, /device:TPU:2, one launch (start us, length us, event | category | flops | bytes accessed | tf_op | source)
XLA Modules:
  0.0 463.6 jit_solution(8965409141635587499)
XLA Ops:
  7.2 27.8 %all_gather.12 = f32[1024,64]{1,0:T(8,128)S(1)} all-gather(f32[32,64]{1,0:T(8,128)} %param.8), channel_id=1, replica_groups=mesh['row'=32,'col'=16] {'row'}, dimensions={0}, use_global_device_ids=true | all-gather | bytes 270336 | tf_op jit(solution)/shard_map/all_gather | solution.py:25
  35.0 0.9 copy.14
  36.0 0.7 all-gather.6.cloned.1.call-update
  36.7 0.7 all-gather.8.cloned.1.call-update
  37.5 77.2 %all-gather.4.cloned.1.call-done = f32[1024,1024]{0,1:T(8,128)} async-done(((f32[1024,64]{0,1:T(8,128)}), f32[1024,1024]{0,1:T(8,128)}) %all-gather.4.cloned.1.call-update) | async-done | bytes 4194320 | tf_op jit(solution)/shard_map/all_gather | solution.py:26
  114.7 4.8 %fusion = f32[1024,1024]{0,1:T(8,128)} fusion(f32[1024,1024]{0,1:T(8,128)} %all-gather.4.cloned.1.call-done), kind=kLoop, calls=%fused_computation.3 | loop fusion | flops 2097152 | bytes 8388608 | tf_op jit(solution)/shard_map/jit(_solve_triangular)/triangular_solve | solution.py:8
  119.5 24.1 %while.1 = (s32[]{:T(128)}, f32[1024,1024]{0,1:T(8,128)}, s32[8,2]{0,1:T(2,128)S(1)}, f32[8,128,128]{2,1,0:T(8,128)S(1)}, s32[]{:T(128)}) while((s32[]{:T(128)}, f32[1024,1024]{0,1:T(8,128)}, s32[8,2]{0,1:T(2,128)S(1)}, f32[8,128,128]{2,1,0:T(8,128)S(1)}, s32[]{:T(128)}) %tuple.28), condition=%wide.while_cond, body=%wide.while_body.sunk | while | flops 2 | bytes 393321 | solution.py:8
  119.5 0.5 fusion.55
  120.1 2.3 dynamic-slice.12
  122.6 0.5 fusion.55
  123.1 2.3 dynamic-slice.12
  125.6 0.5 fusion.55
  126.1 2.3 dynamic-slice.12
  128.6 0.5 fusion.55
  129.1 2.3 dynamic-slice.12
  131.6 0.5 fusion.55
  132.2 2.3 dynamic-slice.12
  134.7 0.5 fusion.55
  135.2 2.3 dynamic-slice.12
  137.7 0.5 fusion.55
  138.2 2.3 dynamic-slice.12
  140.7 0.5 fusion.55
  141.2 2.2 dynamic-slice.12
  143.6 78.6 %custom-call.4 = f32[8,128,128]{1,2,0:T(8,128)S(1)} custom-call(f32[8,128,128]{2,1,0:T(8,128)S(1)} %get-tuple-element.11), custom_call_target="InvertDiagBlocksLowerTriangular" | custom-call | tf_op jit(solution)/shard_map/jit(_solve_triangular)/triangular_solve | solution.py:8
  222.2 1.5 fusion.19
  223.8 1.4 convolution_subtract_fusion.4
  225.1 0.4 fusion.25
  225.5 1.4 convolution_subtract_fusion.3
  227.0 0.4 fusion.26
  227.3 1.6 convolution_subtract_fusion.6
  228.9 0.4 fusion.27
  229.3 1.7 convolution_subtract_fusion.7
  230.9 0.4 constant_dynamic-update-slice_fusion.4
  231.4 1.9 convolution_subtract_fusion.2
  233.3 0.4 constant_dynamic-update-slice_fusion.10
  233.8 2.0 convolution_subtract_fusion.5
  235.9 0.4 constant_dynamic-update-slice_fusion.17
  236.4 2.2 convolution_subtract_fusion.1
  238.6 1.2 convolution_dynamic-update-slice_fusion
  240.1 2.6 fusion.36
  242.7 0.3 reduce-scatter.3.cloned.1.call-start
  243.0 4.8 %fusion.35 = f32[1024,512]{1,0:T(8,128)} fusion(f32[1024,512]{1,0:T(8,128)S(1)} %constant_dynamic-update-slice_fusion.18, f32[512,512]{1,0:T(8,128)S(1)} %copy-done), kind=kOutput, calls=%fused_computation.85 | convolution fusion | flops 3221225472 | bytes 5242880 | tf_op jit(solution)/shard_map/rk,rc->kc/dot_general | solution.py:40
  247.8 0.7 dynamic-slice_bitcast_fusion
  248.5 6.3 %convolution_subtract_fusion = f32[512,512]{1,0:T(8,128)} fusion(f32[512,512]{1,0:T(8,128)} %param.13, f32[1024,512]{1,0:T(8,128)S(1)} %constant_dynamic-update-slice_fusion.18, f32[1024,512]{1,0:T(8,128)} %all-gather.8.cloned.1.call-done), kind=kOutput, calls=%fused_computation.4 | convolution fusion | flops 3221487616 | bytes 6291456 | tf_op jit(solution)/shard_map/dot_general | solution.py:31
  254.9 95.1 %reduce-scatter.5.cloned.1.call-done = f32[32,64]{1,0:T(8,128)} async-done(((f32[1024,64]{1,0:T(8,128)}), f32[32,64]{1,0:T(8,128)}) %reduce-scatter.5.cloned.1.call-update) | async-done | bytes 8208 | tf_op jit(solution)/shard_map/reduce_scatter | solution.py:46
  349.9 1.4 select_subtract_fusion
  351.3 104.3 %reduce-scatter.3.cloned.1.call-done = f32[32,512]{1,0:T(8,128)} async-done(((f32[1024,512]{1,0:T(8,128)}), f32[32,512]{1,0:T(8,128)}) %reduce-scatter.3.cloned.1.call-update) | async-done | bytes 65552 | tf_op jit(solution)/shard_map/reduce_scatter | solution.py:39
  455.6 1.5 sub.10
  (72 shorter events, 2.1 us)
Async XLA Ops:
  7.2 235.8 %copy-start = (f32[512,512]{1,0:T(8,128)S(1)}, f32[512,512]{1,0:T(8,128)}, u32[]{:S(2)}) copy-start(f32[512,512]{1,0:T(8,128)} %param.10) | copy-start | bytes 3145732
  7.2 107.5 %all-gather.4.cloned.1.call-start = ((), (), s32[]{:S(2)}) async-start(), calls=%async_computation.2 | async-start | bytes 4456448 | tf_op jit(solution)/shard_map/all_gather | solution.py:26
  35.9 186.3 %all-gather.6.cloned.1.call-start = ((), (), s32[]{:S(2)}) async-start(), calls=%async_computation.3 | async-start | bytes 2228224 | tf_op jit(solution)/shard_map/all_gather | solution.py:27
  36.7 211.8 %all-gather.8.cloned.1.call-start = ((), (), s32[]{:S(2)}) async-start(), calls=%async_computation.4 | async-start | bytes 2162688 | tf_op jit(solution)/shard_map/all_gather | solution.py:33
  37.4 312.5 %reduce-scatter.5.cloned.1.call-start = ((), (), s32[]{:S(2)}) async-start(), calls=%async_computation.6 | async-start | bytes 540672 | tf_op jit(solution)/shard_map/reduce_scatter | solution.py:46
  222.2 13.7 %copy-start.2 = (f32[8,128,128]{1,2,0:T(8,128)}, f32[8,128,128]{1,2,0:T(8,128)S(1)}, u32[]{:S(2)}) copy-start(f32[8,128,128]{1,2,0:T(8,128)S(1)} %custom-call.4) | copy-start | bytes 1572868
  222.2 5.1 %copy-start.1 = (f32[512,1024]{0,1:T(8,128)S(1)}, f32[512,1024]{0,1:T(8,128)}, u32[]{:S(2)}) copy-start(f32[512,1024]{0,1:T(8,128)} %all-gather.6.cloned.1.call-done) | copy-start | bytes 6291460
  238.6 1.5 copy-start.3
  242.7 212.9 %reduce-scatter.3.cloned.1.call-start = ((), (), s32[]{:S(2)}) async-start(), calls=%async_computation.5 | async-start | bytes 2162688 | tf_op jit(solution)/shard_map/reduce_scatter | solution.py:39
  248.5 101.4 %copy-start.5 = (f32[32,64]{1,0:T(8,128)S(1)}, f32[32,64]{1,0:T(8,128)}, u32[]{:S(2)}) copy-start(f32[32,64]{1,0:T(8,128)} %param.15) | copy-start | bytes 24580
  248.5 207.1 %copy-start.4 = (f32[32,512]{1,0:T(8,128)S(1)}, f32[32,512]{1,0:T(8,128)}, u32[]{:S(2)}) copy-start(f32[32,512]{1,0:T(8,128)} %param.14) | copy-start | bytes 196612
Sparse Core Ops, SparseCore 0:
  36.0 78.6 all-gather.3
  116.8 70.5 all-gather.5
  190.5 55.6 all-gather.7
  250.3 99.5 reduce-scatter.4
  354.2 101.3 reduce-scatter.2
where the time goes:
time: 465 us; the launch traced here: 464 us
  waiting for transfers between devices  278 us (60%)
  other arithmetic  86.2 us (19%)
  matrix products  30.8 us (7%)
  blocking collectives  27.8 us (6%)
  local copies, waits for them, and re-layouts  25.9 us (6%)
  between operations  14.2 us (3%)
    reduce_scatter x1, waiting for transfers between devices, local(): lax.psum_scatter(jnp.einsum('rk,rc->kc', picked, left_factor, precision=h...  104 us
    reduce_scatter x1, waiting for transfers between devices, local(): lax.psum_scatter(jnp.einsum('rk,rc->kc', picked, panel_factor, precision=...  95.1 us
    another operation x3, other arithmetic, right_solve(): jax.scipy.linalg.solve_triangular(tile, source.T, trans='T', lower=True)  83.4 us
    all_gather x1, waiting for transfers between devices, local(): whole_diag = lax.all_gather(column_block, 'col', axis=1, tiled=True)  77.2 us
    all_gather x1, blocking collectives, local(): column_block = lax.all_gather(diag_factor, 'row', axis=0, tiled=True)  27.8 us
    another operation x40, local copies, waits for them, and re-layouts  23.8 us
    another operation x15, matrix products, right_solve(): jax.scipy.linalg.solve_triangular(tile, source.T, trans='T', lower=True)  17.1 us
  transfers between devices with their start and end apart: 5, of which 3 were waited for; matrix products, arithmetic and copies ran while one was open for 30% of the time, Pallas kernels for 0%

commit v1 on v0

--- a/solution.py
+++ b/solution.py
@@ -23,8 +23,13 @@
     my_col = lax.axis_index("col")
     my_row = lax.axis_index("row")
     column_block = lax.all_gather(diag_factor, "row", axis=0, tiled=True)
-    whole_diag = lax.all_gather(column_block, "col", axis=1, tiled=True)
-    full_rows = lax.all_gather(panel_adjoint, "col", axis=1, tiled=True)
+    whole_diag, full_rows = jnp.split(
+        jax.lax.all_gather(
+            jnp.concatenate([column_block, panel_adjoint], 0), axis_name="col", axis=1, tiled=True
+        ),
+        [column_block.shape[0]],
+        0,
+    )
     solved = right_solve(whole_diag, full_rows)
     solved_panel = lax.dynamic_slice_in_dim(solved, my_col * block_width, block_width, 1)
     picked = solved

time: 465 us -> 463 us (level)
    reduce_scatter x1, waiting for transfers between devices: 95.1 us -> 84.4 us  [local(): lax.psum_scatter(jnp.einsum('rk,rc->kc', picked, panel_factor, precision=...]
    all_gather x2 -> x1, waiting for transfers between devices: 77.3 us -> 85.3 us  [local(): jax.lax.all_gather(jnp.concatenate([column_block, panel_adjoint], 0), axi...]
  transfers between devices with their start and end apart: 5 -> 4, of which waited for: 3 -> 3; matrix products, arithmetic and copies ran while one was open for 30% -> 31% of each run, Pallas kernels for 0% -> 0%
where the time goes in v1:
time: 463 us; the launch traced here: 462 us
  waiting for transfers between devices  275 us (59%)
  other arithmetic  86.3 us (19%)
  matrix products  29.4 us (6%)
  local copies, waits for them, and re-layouts  29 us (6%)
  blocking collectives  27.6 us (6%)
  between operations  14.2 us (3%)
    reduce_scatter x1, waiting for transfers between devices, local(): lax.psum_scatter(jnp.einsum('rk,rc->kc', picked, left_factor, precision=h...  104 us
    all_gather x1, waiting for transfers between devices, local(): jax.lax.all_gather(jnp.concatenate([column_block, panel_adjoint], 0), axi...  85.3 us
    reduce_scatter x1, waiting for transfers between devices, local(): lax.psum_scatter(jnp.einsum('rk,rc->kc', picked, panel_factor, precision=...  84.4 us
    another operation x3, other arithmetic, right_solve(): jax.scipy.linalg.solve_triangular(tile, source.T, trans='T', lower=True)  83.4 us
    all_gather x1, blocking collectives, local(): column_block = lax.all_gather(diag_factor, 'row', axis=0, tiled=True)  27.6 us
    another operation x40, local copies, waits for them, and re-layouts  23.8 us
    another operation x15, matrix products, right_solve(): jax.scipy.linalg.solve_triangular(tile, source.T, trans='T', lower=True)  15.7 us
  transfers between devices with their start and end apart: 4, of which 3 were waited for; matrix products, arithmetic and copies ran while one was open for 31% of the time, Pallas kernels for 0%

profile of v1, /device:TPU:2, one launch (start us, length us, event | category | flops | bytes accessed | tf_op | source)
XLA Modules:
  0.0 462.0 jit_solution(16928641645007432970)
XLA Ops:
  7.2 1.1 copy.15
  8.3 27.6 %all_gather.9 = f32[1024,64]{1,0:T(8,128)S(1)} all-gather(f32[32,64]{1,0:T(8,128)} %param.8), channel_id=1, replica_groups=mesh['row'=32,'col'=16] {'row'}, dimensions={0}, use_global_device_ids=true | all-gather | bytes 270336 | tf_op jit(solution)/shard_map/all_gather | solution.py:25
  36.0 1.0 copy.16
  37.1 0.7 all-gather.5.cloned.1.call-update
  37.9 85.3 %all-gather.3.cloned.1.call-done = f32[1536,1024]{0,1:T(8,128)} async-done(((f32[1536,64]{0,1:T(8,128)}), f32[1536,1024]{0,1:T(8,128)}) %all-gather.3.cloned.1.call-update) | async-done | bytes 6291472 | tf_op jit(solution)/shard_map/all_gather | solution.py:27
  123.2 4.8 %slice_select_fusion = f32[1024,1024]{0,1:T(8,128)} fusion(f32[1536,1024]{0,1:T(8,128)} %all-gather.3.cloned.1.call-done), kind=kLoop, calls=%fused_computation.2 | loop fusion | flops 2097152 | bytes 8388608 | tf_op jit(solution)/shard_map/jit(_solve_triangular)/triangular_solve | solution.py:8
  128.0 24.1 %while.1 = (s32[]{:T(128)}, f32[1024,1024]{0,1:T(8,128)}, s32[8,2]{0,1:T(2,128)S(1)}, f32[8,128,128]{2,1,0:T(8,128)S(1)}, s32[]{:T(128)}) while((s32[]{:T(128)}, f32[1024,1024]{0,1:T(8,128)}, s32[8,2]{0,1:T(2,128)S(1)}, f32[8,128,128]{2,1,0:T(8,128)S(1)}, s32[]{:T(128)}) %tuple.28), condition=%wide.while_cond, body=%wide.while_body.sunk | while | flops 2 | bytes 393329 | solution.py:8
  128.1 0.5 fusion.54
  128.6 2.3 dynamic-slice.12
  131.1 0.5 fusion.54
  131.6 2.3 dynamic-slice.12
  134.1 0.5 fusion.54
  134.7 2.3 dynamic-slice.12
  137.2 0.5 fusion.54
  137.7 2.3 dynamic-slice.12
  140.2 0.5 fusion.54
  140.7 2.3 dynamic-slice.12
  143.2 0.5 fusion.54
  143.7 2.3 dynamic-slice.12
  146.2 0.5 fusion.54
  146.8 2.3 dynamic-slice.12
  149.3 0.5 fusion.54
  149.8 2.2 dynamic-slice.12
  152.1 78.6 %custom-call.4 = f32[8,128,128]{1,2,0:T(8,128)S(1)} custom-call(f32[8,128,128]{2,1,0:T(8,128)S(1)} %get-tuple-element.11), custom_call_target="InvertDiagBlocksLowerTriangular" | custom-call | tf_op jit(solution)/shard_map/jit(_solve_triangular)/triangular_solve | solution.py:8
  230.8 2.0 slice_bitcast_fusion
  232.7 0.4 fusion.18
  233.1 1.2 convolution_subtract_fusion.4
  234.3 0.4 fusion.24
  234.7 1.3 convolution_subtract_fusion.3
  236.0 0.4 fusion.25
  236.4 1.6 convolution_subtract_fusion.6
  237.9 0.4 fusion.26
  238.3 1.7 convolution_subtract_fusion.7
  240.0 0.4 constant_dynamic-update-slice_fusion.4
  240.5 1.9 convolution_subtract_fusion.2
  242.4 0.4 constant_dynamic-update-slice_fusion.10
  242.9 2.0 convolution_subtract_fusion.5
  244.9 0.4 constant_dynamic-update-slice_fusion.17
  245.4 2.2 convolution_subtract_fusion.1
  247.7 1.2 convolution_dynamic-update-slice_fusion
  249.1 2.6 fusion.35
  252.1 4.8 %fusion.34 = f32[1024,512]{1,0:T(8,128)} fusion(f32[1024,512]{1,0:T(8,128)S(1)} %constant_dynamic-update-slice_fusion.18, f32[512,512]{1,0:T(8,128)S(1)} %copy-done), kind=kOutput, calls=%fused_computation.87 | convolution fusion | flops 3221225472 | bytes 5242880 | tf_op jit(solution)/shard_map/rk,rc->kc/dot_general | solution.py:45
  256.9 0.7 dynamic-slice_bitcast_fusion
  257.6 6.4 %convolution_subtract_fusion = f32[512,512]{1,0:T(8,128)} fusion(f32[512,512]{1,0:T(8,128)} %param.13, f32[1024,512]{1,0:T(8,128)S(1)} %constant_dynamic-update-slice_fusion.18, f32[1024,512]{1,0:T(8,128)} %all-gather.5.cloned.1.call-done), kind=kOutput, calls=%fused_computation.5 | convolution fusion | flops 3221487616 | bytes 6291456 | tf_op jit(solution)/shard_map/dot_general | solution.py:36
  263.9 84.4 %reduce-scatter.5.cloned.1.call-done = f32[32,64]{1,0:T(8,128)} async-done(((f32[1024,64]{1,0:T(8,128)}), f32[32,64]{1,0:T(8,128)}) %reduce-scatter.5.cloned.1.call-update) | async-done | bytes 8208 | tf_op jit(solution)/shard_map/reduce_scatter | solution.py:51
  348.4 1.4 select_subtract_fusion
  349.8 104.3 %reduce-scatter.3.cloned.1.call-done = f32[32,512]{1,0:T(8,128)} async-done(((f32[1024,512]{1,0:T(8,128)}), f32[32,512]{1,0:T(8,128)}) %reduce-scatter.3.cloned.1.call-update) | async-done | bytes 65552 | tf_op jit(solution)/shard_map/reduce_scatter | solution.py:44
  454.0 1.5 sub.10
  (70 shorter events, 2.4 us)
Async XLA Ops:
  7.2 244.9 %copy-start = (f32[512,512]{1,0:T(8,128)S(1)}, f32[512,512]{1,0:T(8,128)}, u32[]{:S(2)}) copy-start(f32[512,512]{1,0:T(8,128)} %param.10) | copy-start | bytes 3145732
  7.2 116.0 %all-gather.3.cloned.1.call-start = ((), (), s32[]{:S(2)}) async-start(), calls=%async_computation.2 | async-start | bytes 6684672 | tf_op jit(solution)/shard_map/all_gather | solution.py:27
  37.1 220.5 %all-gather.5.cloned.1.call-start = ((), (), s32[]{:S(2)}) async-start(), calls=%async_computation.3 | async-start | bytes 2162688 | tf_op jit(solution)/shard_map/all_gather | solution.py:38
  37.8 310.5 %reduce-scatter.5.cloned.1.call-start = ((), (), s32[]{:S(2)}) async-start(), calls=%async_computation.5 | async-start | bytes 540672 | tf_op jit(solution)/shard_map/reduce_scatter | solution.py:51
  230.7 14.2 %copy-start.1 = (f32[8,128,128]{1,2,0:T(8,128)}, f32[8,128,128]{1,2,0:T(8,128)S(1)}, u32[]{:S(2)}) copy-start(f32[8,128,128]{1,2,0:T(8,128)S(1)} %custom-call.4) | copy-start | bytes 1572868
  247.7 1.5 copy-start.2
  251.8 202.2 %reduce-scatter.3.cloned.1.call-start = ((), (), s32[]{:S(2)}) async-start(), calls=%async_computation.4 | async-start | bytes 2162688 | tf_op jit(solution)/shard_map/reduce_scatter | solution.py:44
  257.5 90.8 %copy-start.4 = (f32[32,64]{1,0:T(8,128)S(1)}, f32[32,64]{1,0:T(8,128)}, u32[]{:S(2)}) copy-start(f32[32,64]{1,0:T(8,128)} %param.15) | copy-start | bytes 24580
  257.6 196.5 %copy-start.3 = (f32[32,512]{1,0:T(8,128)S(1)}, f32[32,512]{1,0:T(8,128)}, u32[]{:S(2)}) copy-start(f32[32,512]{1,0:T(8,128)} %param.14) | copy-start | bytes 196612
Sparse Core Ops, SparseCore 0:
  37.2 85.9 all-gather.2
  126.3 55.6 all-gather.4
  251.9 96.4 reduce-scatter.4
  352.6 101.3 reduce-scatter.2
